TPU v7x, 32 devices: a whole 2x2x4 slice. The times are simulated.
32 devices in a mesh: grp: 2 (over x), dp: 8 (over z, y), layer: 2 (over core).
Axes of the slice: x: 2, y: 2, z: 4, core: 2. Of those that a mesh axis runs over, the one named last changes fastest.
Arguments:
- train_inputs: bfloat16 [128, 4, 32, 4096], P(('grp', 'dp'), 'layer'), parts along dimension 0, may hold values from -6 to 6
- train_grads: bfloat16 [128, 4, 32, 4096], P(('grp', 'dp'), 'layer'), parts along dimension 0, may hold values from -6 to 6
- train_ids: int32 [128, 32], P(('grp', 'dp')), parts along dimension 0, may hold values from 0 to 128001, as said below
- weight_codes: int32 [128, 32], P(('grp', 'dp')), parts along dimension 0, may hold values from 0 to 15
- code_table: float32 [16], replicated, may hold values from -2 to 2
- assignment: int32 [4], replicated, may hold values from 0 to 3, each once
- basis_in: bfloat16 [4, 64, 4096], replicated, may hold values from -0.09375 to 0.09375
- basis_out: bfloat16 [4, 64, 4096], replicated, may hold values from -0.09375 to 0.09375
- query_proj: bfloat16 [256, 16384], P(('grp', 'dp'), 'layer'), parts along dimension 0, may hold values from -0.0078125 to 0.0078125
Outputs:
- scores: float32 [128, 128], P(('dp', 'layer'), 'grp'), parts along dimension 1
- score_tangent: float32 [128, 128], P(('dp', 'layer'), 'grp'), parts along dimension 1
There are 2 independent parts, one for each index of `grp`. A program takes and returns all parts, laid end to end along the dimension named above; an argument that names none is the same for every part. Nothing has to cross between parts.
Inputs may be any that keep to these rules, and one draw needn't show every extreme that they name: `train_ids`: each training example's real tokens come first, at least 8 of them, followed by one or more padding positions holding 128001.
All inputs are finite; a program needn't handle non-finite values.
Results may differ from a plain program's by a relative error of at most 0.005.
Values may be sent and summed in bfloat16 or wider, within the bound.
A program may use at most 128 MiB of HBM per device.

v0:
```python
import jax
import jax.numpy as jnp
from jax import lax
from jax.sharding import PartitionSpec as P

pad_token = 128001


def per_device(
    train_inputs,
    train_grads,
    train_ids,
    weight_codes,
    code_table,
    assignment,
    basis_in,
    basis_out,
    query_proj,
):
    examples, slots, tokens, width = train_inputs.shape
    rank = basis_in.shape[1]
    keep = (train_ids != pad_token).astype(jnp.float32).reshape(-1)
    levels = jnp.arange(code_table.shape[0], dtype=jnp.int32)
    direction = jnp.sum(
        jnp.where(weight_codes[..., None] == levels, code_table, 0.0), axis=-1
    ).reshape(-1)
    first_slot = lax.axis_index("layer") * slots
    plain = []
    tangent = []
    for slot in range(slots):
        layer_id = lax.dynamic_index_in_dim(assignment, first_slot + slot, 0, keepdims=False)
        p_in = lax.dynamic_index_in_dim(basis_in, layer_id, 0, keepdims=False)
        p_out = lax.dynamic_index_in_dim(basis_out, layer_id, 0, keepdims=False)
        rows_x = train_inputs[:, slot].reshape(examples * tokens, width)
        rows_g = train_grads[:, slot].reshape(examples * tokens, width)
        in_proj = jnp.einsum("rd,nd->rn", p_in, rows_x, preferred_element_type=jnp.float32).astype(
            jnp.bfloat16
        )
        out_proj = jnp.einsum("rd,nd->rn", p_out, rows_g, preferred_element_type=jnp.float32)
        kept = (out_proj * keep).astype(jnp.bfloat16)
        weighted = (out_proj * keep * direction).astype(jnp.bfloat16)
        in_three = in_proj.reshape(rank, examples, tokens)
        grad_proj = jnp.einsum(
            "aet,bet->eab",
            kept.reshape(rank, examples, tokens),
            in_three,
            preferred_element_type=jnp.float32,
        )
        grad_tan = jnp.einsum(
            "aet,bet->eab",
            weighted.reshape(rank, examples, tokens),
            in_three,
            preferred_element_type=jnp.float32,
        )
        plain.append(grad_proj.astype(jnp.bfloat16).reshape(examples, rank * rank))
        tangent.append(grad_tan.astype(jnp.bfloat16).reshape(examples, rank * rank))
    grad_all = jnp.concatenate(plain, axis=1)
    tan_all = jnp.concatenate(tangent, axis=1)
    stacked = jnp.stack([grad_all, tan_all])
    partial_scores = jnp.einsum(
        "qf,sef->sqe",
        query_proj,
        lax.all_gather(stacked, "dp", axis=1, tiled=True),
        preferred_element_type=jnp.float32,
    )
    summed = lax.psum_scatter(partial_scores, "layer", scatter_dimension=1, tiled=True)
    return (summed[0], summed[1])


def solution(mesh):
    placed = (
        P(("grp", "dp"), "layer", None, None),
        P(("grp", "dp"), "layer", None, None),
        P(("grp", "dp"), None),
        P(("grp", "dp"), None),
        P(),
        P(),
        P(),
        P(),
        P(("grp", "dp"), "layer"),
    )
    return jax.shard_map(
        per_device,
        mesh=mesh,
        in_specs=placed,
        out_specs=(P(("dp", "layer"), "grp"), P(("dp", "layer"), "grp")),
        check_vma=False,
    )
```

profile of v0, /device:TPU:0, one launch (start us, length us, event | category | flops | bytes accessed | tf_op | source)
XLA Modules:
  0.0 100.8 jit_solution(5889996615391531283)
XLA Ops:
  7.2 0.0 copy-start
  7.2 0.0 all-gather.2.cloned.1.call-start
  7.2 1.4 %fusion.17 = (s32[1]{0:T(128)}, s32[1]{0:T(128)}) fusion(s32[4]{0:T(128)} %param.14, s32[]{:T(128)S(6)} %select_n.20, s32[]{:T(128)S(6)} %select_n.22), kind=kLoop, calls=%fused_computation.36 | loop fusion | bytes 24 | tf_op jit(solution)/shard_map/jit(dynamic_index_in_dim)/dynamic_slice | solution.py:31
  11.2 0.7 compare_convert_fusion
  11.9 0.1 reshape.47
  12.0 0.8 select_reduce_fusion
  12.8 0.1 mul.52
  12.9 4.7 %fusion.13 = (bf16[8,1,32,4096]{3,2,1,0:T(8,128)(2,1)}, bf16[8,1,32,4096]{3,2,1,0:T(8,128)(2,1)}) fusion(bf16[8,2,32,4096]{3,2,1,0:T(8,128)(2,1)} %param.9), kind=kLoop, calls=%fused_computation.32 | loop fusion | bytes 8388608 | tf_op jit(solution)/shard_map/slice | solution.py:34
  18.2 2.5 %convolution_convert_fusion.4 = bf16[64,256]{1,0:T(8,128)(2,1)S(1)} fusion(bf16[256,4096]{1,0:T(8,128)(2,1)} %bitcast.57, bf16[4,64,4096]{2,1,0:T(8,128)(2,1)} %param.15, s32[]{:T(128)S(6)} %select_n.23), kind=kOutput, calls=%fused_computation.6 | convolution fusion | flops 134234112 | bytes 2654212 | tf_op jit(solution)/shard_map/rd,nd->rn/dot_general | solution.py:36
  20.7 0.1 copy.28
  21.5 2.5 %convolution_convert_fusion.5 = bf16[64,256]{1,0:T(8,128)(2,1)S(1)} fusion(bf16[256,4096]{1,0:T(8,128)(2,1)} %bitcast.56, bf16[4,64,4096]{2,1,0:T(8,128)(2,1)} %param.15, s32[]{:T(128)S(6)} %select_n.21), kind=kOutput, calls=%fused_computation.7 | convolution fusion | flops 134234112 | bytes 2654212 | tf_op jit(solution)/shard_map/rd,nd->rn/dot_general | solution.py:36
  24.0 0.1 copy.26
  24.2 2.7 %fusion.14 = (bf16[8,1,32,4096]{3,2,1,0:T(8,128)(2,1)S(1)}, bf16[8,1,32,4096]{3,2,1,0:T(8,128)(2,1)S(1)}) fusion(bf16[8,2,32,4096]{3,2,1,0:T(8,128)(2,1)} %param.10), kind=kLoop, calls=%fused_computation.33 | loop fusion | bytes 8388608 | tf_op jit(solution)/shard_map/slice | solution.py:35
  26.9 0.0 copy-done
  26.9 0.8 fusion.15
  27.7 0.8 fusion.16
  28.4 0.0 copy-start.1
  28.5 0.1 copy.27
  28.6 0.1 copy.25
  28.7 0.2 convolution_convert_fusion.3
  28.9 0.2 reshape.39
  29.1 0.2 convolution_convert_fusion.2
  29.4 0.2 reshape.42
  29.5 0.1 copy.30
  29.7 0.2 convolution_convert_fusion
  29.9 0.2 reshape.46
  30.1 0.1 copy.29
  30.2 0.2 convolution_convert_fusion.1
  30.4 0.2 reshape.44
  30.7 0.7 pad_maximum_fusion
  31.4 0.0 all-gather.2.cloned.1.call-update
  31.4 0.0 reduce-scatter.2.cloned.1.call-start
  31.4 52.1 %all-gather.2.cloned.1.call-done = bf16[2,64,8192]{2,1,0:T(8,128)(2,1)} async-done(((bf16[2,8,8192]{2,1,0:T(8,128)(2,1)}), bf16[2,64,8192]{2,1,0:T(8,128)(2,1)}) %all-gather.2.cloned.1.call-update) | async-done | bytes 2097168 | tf_op jit(solution)/shard_map/all_gather | solution.py:63
  83.5 0.0 copy-done.1
  83.5 3.1 %convolution_bitcast_fusion = f32[2,16,64]{2,1,0:T(8,128)} fusion(bf16[2,64,8192]{2,1,0:T(8,128)(2,1)} %all-gather.2.cloned.1.call-done, bf16[16,8192]{1,0:T(8,128)(2,1)S(1)} %copy-done.1), kind=kOutput, calls=%fused_computation.8 | convolution fusion | flops 33554432 | bytes 2367488 | tf_op jit(solution)/shard_map/qf,sef->sqe/dot_general | solution.py:60
  86.6 0.0 reduce-scatter.2.cloned.1.call-update
  86.7 6.0 %reduce-scatter.2.cloned.1.call-done = f32[2,8,64]{2,1,0:T(8,128)} async-done(((f32[2,16,64]{2,1,0:T(8,128)}), f32[2,8,64]{2,1,0:T(8,128)}) %reduce-scatter.2.cloned.1.call-update) | async-done | bytes 4112 | tf_op jit(solution)/shard_map/reduce_scatter | solution.py:66
  92.7 1.3 %slice_bitcast_fusion = (f32[8,64]{1,0:T(8,128)}, f32[8,64]{1,0:T(8,128)}) fusion(f32[2,8,64]{2,1,0:T(8,128)} %reduce-scatter.2.cloned.1.call-done), kind=kLoop, calls=%fused_computation.25 | loop fusion | bytes 8192 | tf_op jit(solution)/shard_map/squeeze | solution.py:67
  (1 shorter events, 0.0 us)
Async XLA Ops:
  7.2 19.7 %copy-start = (bf16[4,64,4096]{2,1,0:T(8,128)(2,1)S(1)}, bf16[4,64,4096]{2,1,0:T(8,128)(2,1)}, u32[]{:S(2)}) copy-start(bf16[4,64,4096]{2,1,0:T(8,128)(2,1)} %param.16) | copy-start | bytes 6291460
  7.2 76.3 %all-gather.2.cloned.1.call-start = ((), (), s32[]{:S(2)}) async-start(), calls=%async_computation.1 | async-start | bytes 2359296 | tf_op jit(solution)/shard_map/all_gather | solution.py:63
  28.4 55.1 %copy-start.1 = (bf16[16,8192]{1,0:T(8,128)(2,1)S(1)}, bf16[16,8192]{1,0:T(8,128)(2,1)}, u32[]{:S(2)}) copy-start(bf16[16,8192]{1,0:T(8,128)(2,1)} %param.17) | copy-start | bytes 786436
  31.4 61.3 %reduce-scatter.2.cloned.1.call-start = ((), (), s32[]{:S(2)}) async-start(), calls=%async_computation.2 | async-start | bytes 24576 | tf_op jit(solution)/shard_map/reduce_scatter | solution.py:66
Sparse Core Ops, SparseCore 0:
  31.5 51.9 all-gather.1
  86.8 5.8 reduce-scatter.1
where the time goes:
time: 101 us
  waiting for transfers between devices  58.1 us (58%)
  between operations  18.1 us (18%)
  local copies, waits for them, and re-layouts  11.6 us (11%)
  matrix products  10.7 us (11%)
  other arithmetic  2.22 us (2%)
    all_gather x1, waiting for transfers between devices, per_device(): lax.all_gather(stacked, 'dp', axis=1, tiled=True)  52.1 us
    reduce_scatter x1, waiting for transfers between devices, per_device(): lax.psum_scatter(partial_scores, 'layer', scatter_dimension=1, tiled=True)  6.04 us
    dot_general x2, matrix products, per_device(): jnp.einsum('rd,nd->rn', p_in, rows_x, preferred_element_type=jnp.float32)  5.06 us
    slice x1, local copies, waits for them, and re-layouts, per_device(): rows_x = train_inputs[:, slot].reshape(examples * tokens, width)  4.67 us
    dot_general x1, matrix products, per_device(): jnp.einsum('qf,sef->sqe', query_proj, lax.all_gather(stacked, 'dp', axis=...  3.12 us
    slice x1, local copies, waits for them, and re-layouts, per_device(): rows_g = train_grads[:, slot].reshape(examples * tokens, width)  2.71 us
  transfers between devices with their start and end apart: 2, of which 2 were waited for; matrix products, arithmetic and copies ran while one was open for 0% of the time, Pallas kernels for 0%

commit v1 on v0

v1 whole, which is shorter than its diff:
```python
import functools

import jax
import jax.numpy as jnp
from jax import lax
from jax.experimental import pallas as pl
from jax.experimental.pallas import tpu as pltpu
from jax.sharding import PartitionSpec as P

pad_token = 128001
MESH = pl.DeviceIdType.MESH
NT = (((1,), (1,)), ((), ()))


def loop(count, body):
    if count <= 4:
        for step in range(count):
            body(step)
    else:
        lax.fori_loop(0, count, lambda step, carry: (body(step), carry)[1], 0)


def kernel(
    blocks, x_hbm, g_hbm, ids_ref, codes_ref, table_ref, assign_ref, bin_hbm, bout_hbm, q_hbm,
    out_ref,
    x_buf, g_buf, bin_buf, bout_buf, q_buf, in_own, kept_own, in_all, kept_all, kept_wide, grads, part, sums,
    load_sem, basis_sem, q_send, q_recv, relay_send, in_send, kept_send, in_recv, kept_recv, sum_send, sum_recv,
):
    examples, slots, tokens, width = x_hbm.shape
    chips, rank = bin_hbm.shape[:2]
    lanes = examples * tokens
    features = rank * rank
    cores = chips // slots
    kinds = 2 * examples
    share = q_hbm.shape[0] // cores
    grp_dp = lax.axis_index("dp")
    core = lax.axis_index("layer")
    block = grp_dp // chips
    chip = lax.rem(grp_dp, chips)
    base = block * chips

    load_bin = pltpu.make_async_copy(bin_hbm, bin_buf, basis_sem.at[0])
    load_bout = pltpu.make_async_copy(bout_hbm, bout_buf, basis_sem.at[1])
    loads_x = [pltpu.make_async_copy(x_hbm.at[:, k], x_buf.at[k], load_sem.at[k, 0]) for k in range(slots)]
    loads_g = [pltpu.make_async_copy(g_hbm.at[:, k], g_buf.at[k], load_sem.at[k, 1]) for k in range(slots)]
    load_bin.start()
    loads_x[0].start()
    load_bout.start()
    loads_g[0].start()
    for k in range(1, slots):
        loads_x[k].start()
        loads_g[k].start()

    barrier = pltpu.get_barrier_semaphore()
    for other in range(1, chips * cores):
        place = lax.rem(chip * cores + core + other, chips * cores)
        pl.semaphore_signal(
            barrier, inc=1, device_id={"dp": base + place // cores, "layer": lax.rem(place, cores)}, device_id_type=MESH
        )

    def greet(step):
        far = lax.rem(block + step + 1, blocks) * chips
        for k in range(slots):
            pl.semaphore_signal(
                barrier, inc=1, device_id={"dp": far + k * cores + core, "layer": chip // slots}, device_id_type=MESH
            )

    loop(blocks - 1, greet)
    pl.semaphore_wait(barrier, chips * cores - 1 + slots * (blocks - 1))

    to_core = lax.rem(chip, cores)
    slot_of = [core * slots + k for k in range(slots)]
    stays = [jnp.logical_and(chip == slot_of[k], to_core == core) for k in range(slots)]

    def q_copy(k):
        return pltpu.make_async_remote_copy(
            src_ref=q_hbm.at[:, pl.ds(k * features, features)],
            dst_ref=q_buf.at[chip],
            send_sem=q_send.at[k],
            recv_sem=q_recv.at[chip],
            device_id={"dp": base + slot_of[k], "layer": to_core},
            device_id_type=MESH,
        )

    for k in range(slots):

        @pl.when(jnp.logical_not(stays[k]))
        def _():
            q_copy(k).start()

        @pl.when(stays[k])
        def _():
            pltpu.make_async_copy(
                q_hbm.at[:, pl.ds(k * features, features)], q_buf.at[chip], q_recv.at[chip]
            ).start()

    ids = ids_ref[...]
    codes = codes_ref[...]
    keep8 = (ids != pad_token).astype(jnp.float32)
    dir8 = jnp.zeros(codes.shape, jnp.float32)
    for code in range(table_ref.shape[0]):
        dir8 = jnp.where(codes == code, table_ref[code], dir8)
    keep = jnp.concatenate([keep8[e : e + 1] for e in range(examples)], axis=1)
    direction = jnp.concatenate([dir8[e : e + 1] for e in range(examples)], axis=1)
    dir_high = direction.astype(jnp.bfloat16).astype(jnp.float32)
    dir_low = direction - dir_high
    row16 = lax.broadcasted_iota(jnp.int32, (16, lanes), 0)
    dir_rows = jnp.where(row16 == 0, dir_high, jnp.where(row16 == 1, dir_low, 0.0)).astype(jnp.bfloat16)

    mine = block * slots + chip // cores

    def factor_copy(k, far_block, own, every, send, recv):
        return pltpu.make_async_remote_copy(
            src_ref=own.at[k],
            dst_ref=every.at[mine],
            send_sem=send.at[k, far_block],
            recv_sem=recv.at[mine],
            device_id={"dp": far_block * chips + slot_of[k], "layer": to_core},
            device_id_type=MESH,
        )

    def send_factor(k, own, every, send, recv):
        def far(step):
            factor_copy(k, lax.rem(block + step + 1, blocks), own, every, send, recv).start()

        loop(blocks - 1, far)

        @pl.when(jnp.logical_not(stays[k]))
        def _():
            factor_copy(k, block, own, every, send, recv).start()

        @pl.when(stays[k])
        def _():
            pltpu.make_async_copy(own.at[k], every.at[mine], recv.at[mine]).start()

    def sent_factor(k, own, every, send, recv):
        def far(step):
            factor_copy(k, lax.rem(block + step + 1, blocks), own, every, send, recv).wait_send()

        loop(blocks - 1, far)

        @pl.when(jnp.logical_not(stays[k]))
        def _():
            factor_copy(k, block, own, every, send, recv).wait_send()

    def relay(h):
        source = h * cores + core
        return pltpu.make_async_remote_copy(
            src_ref=q_buf.at[source],
            dst_ref=q_buf.at[source],
            send_sem=relay_send.at[h],
            recv_sem=q_recv.at[source],
            device_id={"layer": 1 - core},
            device_id_type=MESH,
        )

    in_args = (in_own, in_all, in_send, in_recv)
    kept_args = (kept_own, kept_all, kept_send, kept_recv)
    for k in range(slots):
        layer_id = assign_ref[core * slots + k]
        if k == 0:
            load_bin.wait()
        loads_x[k].wait()
        in_proj = lax.dot_general(
            bin_buf[layer_id], x_buf[k].reshape(lanes, width), NT, preferred_element_type=jnp.float32
        )
        in_own[k] = in_proj.astype(jnp.bfloat16)
        send_factor(k, *in_args)
        if k == 0:
            load_bout.wait()
        loads_g[k].wait()
        out_proj = lax.dot_general(
            bout_buf[layer_id], g_buf[k].reshape(lanes, width), NT, preferred_element_type=jnp.float32
        )
        kept_own[k, :rank] = (out_proj * keep).astype(jnp.bfloat16)
        kept_own[k, rank:] = dir_rows
        send_factor(k, *kept_args)

    for h in range(chips // cores):
        relay(h).wait_recv()
        relay(h).start()

    row = lax.broadcasted_iota(jnp.int32, (kinds, lanes), 0)
    lane = lax.broadcasted_iota(jnp.int32, (kinds, lanes), 1)
    own_tokens = lane // tokens == lax.rem(row, examples)
    group = 256 // rank

    def product(step):
        near = lax.rem(block + step // (chips // cores), blocks)
        at = near * (chips // cores) + lax.rem(step, chips // cores)
        pltpu.make_async_copy(in_all.at[at], in_all.at[at], in_recv.at[at]).wait()
        pltpu.make_async_copy(kept_all.at[at], kept_all.at[at], kept_recv.at[at]).wait()
        in_block = in_all[at]
        kept_wide[...] = kept_all[at].astype(jnp.float32)
        dirs = kept_wide[rank : rank + 1] + kept_wide[rank + 1 : rank + 2]
        scale = jnp.where(own_tokens, jnp.where(row < examples, 1.0, dirs), 0.0)
        total = None
        for i in range(group):
            left = jnp.concatenate(
                [
                    (kept_wide[a : a + 1] * scale).astype(jnp.bfloat16)
                    for a in range(i, rank, group)
                ],
                axis=0,
            )
            pieces = [jnp.zeros_like(in_block)] * group
            pieces[i] = in_block
            right = jnp.concatenate(pieces, axis=0)
            term = lax.dot_general(left, right, NT, preferred_element_type=jnp.float32)
            total = term if total is None else total + term
        rounded = total.astype(jnp.bfloat16)
        flat = jnp.concatenate(
            [rounded[a * kinds : (a + 1) * kinds] for a in range(rank // group)], axis=1
        )
        grads[pl.ds(pl.multiple_of(at * kinds, kinds), kinds)] = flat

    count = blocks * (chips // cores)
    loop(count, product)

    for h in range(chips // cores):
        source = h * cores + 1 - core
        pltpu.make_async_copy(q_buf.at[source], q_buf.at[source], q_recv.at[source]).wait()
    scores = lax.dot_general(
        q_buf[...].reshape(chips * q_buf.shape[1], features), grads[...], NT, preferred_element_type=jnp.float32
    )
    for place in range(chips * cores):
        part[place] = scores[place * share : (place + 1) * share]

    here = chip * cores + core

    def sum_copy(other):
        place = lax.rem(here + other, chips * cores)
        return pltpu.make_async_remote_copy(
            src_ref=part.at[place],
            dst_ref=sums.at[here],
            send_sem=sum_send.at[other],
            recv_sem=sum_recv.at[here],
            device_id={"dp": base + place // cores, "layer": lax.rem(place, cores)},
            device_id_type=MESH,
        )

    for other in range(1, chips * cores):
        sum_copy(other).start()
    pltpu.make_async_copy(part.at[here], sums.at[here], sum_recv.at[here]).start()
    for place in range(chips * cores):
        pltpu.make_async_copy(sums.at[place], sums.at[place], sum_recv.at[place]).wait()
    for c in range(cores):
        total = sums[c]
        for j in range(1, chips):
            total = total + sums[j * cores + c]
        out_ref[c] = total

    for k in range(slots):

        @pl.when(jnp.logical_not(stays[k]))
        def _():
            q_copy(k).wait_send()

        sent_factor(k, *in_args)
        sent_factor(k, *kept_args)
    for h in range(chips // cores):
        relay(h).wait_send()
    for other in range(1, chips * cores):
        sum_copy(other).wait_send()


def per_device(blocks, x, g, ids, codes, table, assignment, basis_in, basis_out, query):
    examples, slots, tokens, width = x.shape
    chips, rank = basis_in.shape[:2]
    cores = chips // slots
    lanes = examples * tokens
    features = rank * rank
    count = blocks * (chips // cores)
    kinds = 2 * examples
    queries = query.shape[0]
    share = queries // cores
    any_spec = pl.BlockSpec(memory_space=pl.ANY)
    vmem = pl.BlockSpec(memory_space=pltpu.VMEM)
    smem = pl.BlockSpec(memory_space=pltpu.SMEM)
    bf16, f32 = jnp.bfloat16, jnp.float32
    dma = pltpu.SemaphoreType.DMA
    summed = pl.pallas_call(
        functools.partial(kernel, blocks),
        out_shape=jax.ShapeDtypeStruct((cores, share, count * kinds), f32),
        in_specs=[any_spec, any_spec, vmem, vmem, smem, smem, any_spec, any_spec, any_spec],
        out_specs=vmem,
        scratch_shapes=[
            pltpu.VMEM((slots, examples, tokens, width), bf16),
            pltpu.VMEM((slots, examples, tokens, width), bf16),
            pltpu.VMEM(basis_in.shape, bf16),
            pltpu.VMEM(basis_out.shape, bf16),
            pltpu.VMEM((chips, queries, features), bf16),
            pltpu.VMEM((slots, rank, lanes), bf16),
            pltpu.VMEM((slots, rank + 16, lanes), bf16),
            pltpu.VMEM((count, rank, lanes), bf16),
            pltpu.VMEM((count, rank + 16, lanes), bf16),
            pltpu.VMEM((rank + 16, lanes), f32),
            pltpu.VMEM((count * kinds, features), bf16),
            pltpu.VMEM((chips * cores, share, count * kinds), f32),
            pltpu.VMEM((chips * cores, share, count * kinds), f32),
            dma((slots, 2)),
            dma((2,)),
            dma((slots,)),
            dma((chips,)),
            dma((chips // cores,)),
            dma((slots, blocks)),
            dma((slots, blocks)),
            dma((count,)),
            dma((count,)),
            dma((chips * cores,)),
            dma((chips * cores,)),
        ],
        compiler_params=pltpu.CompilerParams(
            collective_id=0, has_side_effects=True, vmem_limit_bytes=48 * 1024 * 1024
        ),
    )(x, g, ids, codes, table, assignment, basis_in, basis_out, query)
    split = summed.reshape(cores, share, count, 2, examples).transpose(3, 1, 2, 0, 4)
    split = split.reshape(2, share, count * cores * examples)
    return split[0], split[1]


def solution(mesh):
    placed = (
        P(("grp", "dp"), "layer", None, None),
        P(("grp", "dp"), "layer", None, None),
        P(("grp", "dp"), None),
        P(("grp", "dp"), None),
        P(),
        P(),
        P(),
        P(),
        P(("grp", "dp"), "layer"),
    )

    def run(*args):
        chips = args[5].shape[0]
        return jax.shard_map(
            functools.partial(per_device, mesh.shape["dp"] // chips),
            mesh=mesh,
            in_specs=placed,
            out_specs=(P(("dp", "layer"), "grp"), P(("dp", "layer"), "grp")),
            check_vma=False,
        )(*args)

    return run
```

time: 101 us -> 31.9 us (0.32)
  waiting for transfers between devices: 58.1 us -> 0 us
  Pallas kernels: 0 us -> 22.5 us
  between operations: 18.1 us -> 0.68 us
  matrix products: 10.7 us -> 0 us
  local copies, waits for them, and re-layouts: 11.6 us -> 8.43 us
  other arithmetic: 2.22 us -> 0 us
    all_gather x1 -> x0, waiting for transfers between devices: 52.1 us -> none  [per_device(): lax.all_gather(stacked, 'dp', axis=1, tiled=True)]
    pallas_call x0 -> x1, Pallas kernels: none -> 22.5 us  [per_device(): pl.pallas_call(functools.partial(kernel, blocks), out_shape=jax.ShapeDtyp...]
    dot_general x9 -> x0, matrix products: 10.7 us -> none  [the longest x2 5.06 us: per_device(): jnp.einsum('rd,nd->rn', p_in, rows_x, preferred_element_type=jnp.float32)]
    slice x2 -> x3, local copies, waits for them, and re-layouts: 7.38 us -> 0.11 us  [per_device(): return (split[0], split[1])]
    unnamed x4 -> x14, local copies, waits for them, and re-layouts: 0.01 us -> 6.81 us
    reduce_scatter x1 -> x0, waiting for transfers between devices: 6.04 us -> none  [per_device(): lax.psum_scatter(partial_scores, 'layer', scatter_dimension=1, tiled=True)]
    dynamic_slice x1 -> x0, local copies, waits for them, and re-layouts: 1.4 us -> none  [per_device(): lax.dynamic_index_in_dim(assignment, first_slot + slot, 0, keepdims=False)]
  transfers between devices with their start and end apart: 2 -> 0, of which waited for: 2 -> 0; matrix products, arithmetic and copies ran while one was open for 0% -> 0% of each run, Pallas kernels for 0% -> 0%
where the time goes in v1:
time: 31.9 us; the launch traced here: 31.6 us
  Pallas kernels  22.5 us (71%)
  local copies, waits for them, and re-layouts  8.43 us (26%)
  between operations  0.68 us (2%)
    pallas_call x1, Pallas kernels, per_device(): pl.pallas_call(functools.partial(kernel, blocks), out_shape=jax.ShapeDtyp...  22.5 us
    unnamed x14, local copies, waits for them, and re-layouts  6.81 us
    squeeze x2, local copies, waits for them, and re-layouts, per_device(): return (split[0], split[1])  1.39 us

profile of v1, /device:TPU:0, one launch (start us, length us, event | category | flops | bytes accessed | tf_op | source)
XLA Modules:
  0.0 31.6 jit_solution(1597161125817192044)
XLA Ops:
  0.6 0.0 copy-start
  0.6 1.6 %copy-done = bf16[4,64,4096]{2,1,0:T(8,128)(2,1)S(1)} copy-done((bf16[4,64,4096]{2,1,0:T(8,128)(2,1)S(1)}, bf16[4,64,4096]{2,1,0:T(8,128)(2,1)}, u32[]{:S(2)}) %copy-start) | copy-done | bytes 2097176
  2.2 0.0 copy-start.1
  2.2 1.6 %copy-done.1 = bf16[4,64,4096]{2,1,0:T(8,128)(2,1)S(1)} copy-done((bf16[4,64,4096]{2,1,0:T(8,128)(2,1)S(1)}, bf16[4,64,4096]{2,1,0:T(8,128)(2,1)}, u32[]{:S(2)}) %copy-start.1) | copy-done | bytes 2097176
  3.8 0.0 copy-start.2
  3.8 0.9 %copy-done.2 = bf16[16,8192]{1,0:T(8,128)(2,1)S(1)} copy-done((bf16[16,8192]{1,0:T(8,128)(2,1)S(1)}, bf16[16,8192]{1,0:T(8,128)(2,1)}, u32[]{:S(2)}) %copy-start.2) | copy-done | bytes 262168
  4.8 0.0 copy-start.3
  4.8 0.7 %copy-done.3 = s32[8,32]{1,0:T(8,128)S(1)} copy-done((s32[8,32]{1,0:T(8,128)S(1)}, s32[8,32]{1,0:T(8,128)}, u32[]{:S(2)}) %copy-start.3) | copy-done | bytes 1048
  5.5 0.0 copy-start.4
  5.5 0.7 %copy-done.4 = s32[8,32]{1,0:T(8,128)S(1)} copy-done((s32[8,32]{1,0:T(8,128)S(1)}, s32[8,32]{1,0:T(8,128)}, u32[]{:S(2)}) %copy-start.4) | copy-done | bytes 1048
  6.1 0.0 copy-start.5
  6.1 0.7 %copy-done.5 = f32[16]{0:T(128)S(1)} copy-done((f32[16]{0:T(128)S(1)}, f32[16]{0:T(128)}, u32[]{:S(2)}) %copy-start.5) | copy-done | bytes 88
  6.8 0.0 copy-start.6
  6.8 0.7 %copy-done.6 = s32[4]{0:T(128)S(1)} copy-done((s32[4]{0:T(128)S(1)}, s32[4]{0:T(128)}, u32[]{:S(2)}) %copy-start.6) | copy-done | bytes 40
  7.5 22.5 %shard_map.104 = f32[2,8,64]{2,1,0:T(8,128)S(1)} custom-call(bf16[8,2,32,4096]{3,2,1,0:T(8,128)(2,1)} %x_hbm.1, bf16[8,2,32,4096]{3,2,1,0:T(8,128)(2,1)} %g_hbm.1, s32[8,32]{1,0:T(8,128)S(1)} %copy-done.3, s32[8,32]{1,0:T(8,128)S(1)} %copy-done.4, f32[16]{0:T(128)S(1)} %copy-done.5, s32[4]{0:T(128)S(1)} %copy-done.6, bf16[4,64,4096]{2,1,0:T(8,128)(2,1)S(1)} %copy-done, ...), custom_call_target="tpu_custom_call" | custom-call | tf_op jit(solution)/shard_map/pallas_call | solution.py:282
  29.9 0.1 reshape.12
  30.1 0.1 fusion
  30.1 0.7 %squeeze.7 = f32[8,64]{1,0:T(8,128)} reshape(f32[1,8,4,2,8]{4,3,2,1,0:T(2,128)S(1)} %copy.12) | data formatting | bytes 4096 | tf_op jit(solution)/shard_map/squeeze | solution.py:319
  30.9 0.7 %squeeze.6 = f32[8,64]{1,0:T(8,128)} reshape(f32[1,8,4,2,8]{4,3,2,1,0:T(2,128)S(1)} %copy.11) | data formatting | bytes 4096 | tf_op jit(solution)/shard_map/squeeze | solution.py:319
  (2 shorter events, 0.1 us)
Async XLA Ops:
  0.6 1.6 %copy-start = (bf16[4,64,4096]{2,1,0:T(8,128)(2,1)S(1)}, bf16[4,64,4096]{2,1,0:T(8,128)(2,1)}, u32[]{:S(2)}) copy-start(bf16[4,64,4096]{2,1,0:T(8,128)(2,1)} %bin_hbm.1) | copy-start | bytes 6291460
  2.2 1.6 %copy-start.1 = (bf16[4,64,4096]{2,1,0:T(8,128)(2,1)S(1)}, bf16[4,64,4096]{2,1,0:T(8,128)(2,1)}, u32[]{:S(2)}) copy-start(bf16[4,64,4096]{2,1,0:T(8,128)(2,1)} %bout_hbm.1) | copy-start | bytes 6291460
  3.8 0.9 %copy-start.2 = (bf16[16,8192]{1,0:T(8,128)(2,1)S(1)}, bf16[16,8192]{1,0:T(8,128)(2,1)}, u32[]{:S(2)}) copy-start(bf16[16,8192]{1,0:T(8,128)(2,1)} %q_hbm.1) | copy-start | bytes 786436
  4.8 0.7 %copy-start.3 = (s32[8,32]{1,0:T(8,128)S(1)}, s32[8,32]{1,0:T(8,128)}, u32[]{:S(2)}) copy-start(s32[8,32]{1,0:T(8,128)} %ids_ref.1) | copy-start | bytes 3076
  5.5 0.7 %copy-start.4 = (s32[8,32]{1,0:T(8,128)S(1)}, s32[8,32]{1,0:T(8,128)}, u32[]{:S(2)}) copy-start(s32[8,32]{1,0:T(8,128)} %codes_ref.1) | copy-start | bytes 3076
  6.1 0.7 %copy-start.5 = (f32[16]{0:T(128)S(1)}, f32[16]{0:T(128)}, u32[]{:S(2)}) copy-start(f32[16]{0:T(128)} %table_ref.1) | copy-start | bytes 196
  6.8 0.7 %copy-start.6 = (s32[4]{0:T(128)S(1)}, s32[4]{0:T(128)}, u32[]{:S(2)}) copy-start(s32[4]{0:T(128)} %assign_ref.1) | copy-start | bytes 52

commit v2 on v1

--- a/solution.py
+++ b/solution.py
@@ -21,10 +21,11 @@
 
 
 def kernel(
-    blocks, x_hbm, g_hbm, ids_ref, codes_ref, table_ref, assign_ref, bin_hbm, bout_hbm, q_hbm,
-    out_ref,
+    blocks, x_hbm, g_hbm, ids_hbm, codes_hbm, table_hbm, assign_hbm, bin_hbm, bout_hbm, q_hbm,
+    scores_hbm, tangent_hbm,
     x_buf, g_buf, bin_buf, bout_buf, q_buf, in_own, kept_own, in_all, kept_all, kept_wide, grads, part, sums,
-    load_sem, basis_sem, q_send, q_recv, relay_send, in_send, kept_send, in_recv, kept_recv, sum_send, sum_recv,
+    ids_ref, codes_ref, table_ref, assign_ref, result,
+    load_sem, basis_sem, q_send, q_recv, relay_send, in_send, kept_send, in_recv, kept_recv, sum_send, sum_recv, small_sem, result_sem,
 ):
     examples, slots, tokens, width = x_hbm.shape
     chips, rank = bin_hbm.shape[:2]
@@ -43,6 +44,14 @@
     load_bout = pltpu.make_async_copy(bout_hbm, bout_buf, basis_sem.at[1])
     loads_x = [pltpu.make_async_copy(x_hbm.at[:, k], x_buf.at[k], load_sem.at[k, 0]) for k in range(slots)]
     loads_g = [pltpu.make_async_copy(g_hbm.at[:, k], g_buf.at[k], load_sem.at[k, 1]) for k in range(slots)]
+    smalls = [
+        pltpu.make_async_copy(source, target, small_sem.at[at])
+        for at, (source, target) in enumerate(
+            ((assign_hbm, assign_ref), (table_hbm, table_ref), (ids_hbm, ids_ref), (codes_hbm, codes_ref))
+        )
+    ]
+    for small in smalls:
+        small.start()
     load_bin.start()
     loads_x[0].start()
     load_bout.start()
@@ -94,6 +103,8 @@
                 q_hbm.at[:, pl.ds(k * features, features)], q_buf.at[chip], q_recv.at[chip]
             ).start()
 
+    for small in smalls:
+        small.wait()
     ids = ids_ref[...]
     codes = codes_ref[...]
     keep8 = (ids != pad_token).astype(jnp.float32)
@@ -244,11 +255,27 @@
     pltpu.make_async_copy(part.at[here], sums.at[here], sum_recv.at[here]).start()
     for place in range(chips * cores):
         pltpu.make_async_copy(sums.at[place], sums.at[place], sum_recv.at[place]).wait()
+    by_core = []
     for c in range(cores):
         total = sums[c]
         for j in range(1, chips):
             total = total + sums[j * cores + c]
-        out_ref[c] = total
+        by_core.append(total)
+    for kind in range(2):
+        result[kind] = jnp.concatenate(
+            [
+                total[:, at * kinds + kind * examples : at * kinds + (kind + 1) * examples]
+                for at in range(count)
+                for total in by_core
+            ],
+            axis=1,
+        )
+    results = [
+        pltpu.make_async_copy(result.at[kind], target, result_sem.at[kind])
+        for kind, target in enumerate((scores_hbm, tangent_hbm))
+    ]
+    for copy in results:
+        copy.start()
 
     for k in range(slots):
 
@@ -262,6 +289,8 @@
         relay(h).wait_send()
     for other in range(1, chips * cores):
         sum_copy(other).wait_send()
+    for copy in results:
+        copy.wait()
 
 
 def per_device(blocks, x, g, ids, codes, table, assignment, basis_in, basis_out, query):
@@ -274,16 +303,14 @@
     kinds = 2 * examples
     queries = query.shape[0]
     share = queries // cores
-    any_spec = pl.BlockSpec(memory_space=pl.ANY)
-    vmem = pl.BlockSpec(memory_space=pltpu.VMEM)
-    smem = pl.BlockSpec(memory_space=pltpu.SMEM)
+    hbm = pl.BlockSpec(memory_space=pltpu.HBM)
     bf16, f32 = jnp.bfloat16, jnp.float32
     dma = pltpu.SemaphoreType.DMA
-    summed = pl.pallas_call(
+    return pl.pallas_call(
         functools.partial(kernel, blocks),
-        out_shape=jax.ShapeDtypeStruct((cores, share, count * kinds), f32),
-        in_specs=[any_spec, any_spec, vmem, vmem, smem, smem, any_spec, any_spec, any_spec],
-        out_specs=vmem,
+        out_shape=(jax.ShapeDtypeStruct((share, count * cores * examples), f32),) * 2,
+        in_specs=[hbm] * 9,
+        out_specs=(hbm, hbm),
         scratch_shapes=[
             pltpu.VMEM((slots, examples, tokens, width), bf16),
             pltpu.VMEM((slots, examples, tokens, width), bf16),
@@ -298,6 +325,11 @@
             pltpu.VMEM((count * kinds, features), bf16),
             pltpu.VMEM((chips * cores, share, count * kinds), f32),
             pltpu.VMEM((chips * cores, share, count * kinds), f32),
+            pltpu.VMEM(ids.shape, jnp.int32),
+            pltpu.VMEM(codes.shape, jnp.int32),
+            pltpu.SMEM(table.shape, f32),
+            pltpu.SMEM(assignment.shape, jnp.int32),
+            pltpu.VMEM((2, share, count * cores * examples), f32),
             dma((slots, 2)),
             dma((2,)),
             dma((slots,)),
@@ -309,14 +341,13 @@
             dma((count,)),
             dma((chips * cores,)),
             dma((chips * cores,)),
+            dma((4,)),
+            dma((2,)),
         ],
         compiler_params=pltpu.CompilerParams(
             collective_id=0, has_side_effects=True, vmem_limit_bytes=48 * 1024 * 1024
         ),
-    )(x, g, ids, codes, table, assignment, basis_in, basis_out, query)
-    split = summed.reshape(cores, share, count, 2, examples).transpose(3, 1, 2, 0, 4)
-    split = split.reshape(2, share, count * cores * examples)
-    return split[0], split[1]
+    )(*[pltpu.with_memory_space_constraint(a, pltpu.HBM) for a in (x, g, ids, codes, table, assignment, basis_in, basis_out, query)])
 
 
 def solution(mesh):

time: 31.9 us -> 24 us (0.75)
  local copies, waits for them, and re-layouts: 8.43 us -> 1.19 us
  Pallas kernels: 22.5 us -> 22 us
    unnamed x14 -> x2, local copies, waits for them, and re-layouts: 6.81 us -> 1.19 us
    squeeze x2 -> x0, local copies, waits for them, and re-layouts: 1.39 us -> none  [per_device(): return (split[0], split[1])]
    pallas_call x1, Pallas kernels: 22.5 us -> 22 us  [per_device(): pl.pallas_call(functools.partial(kernel, blocks), out_shape=(jax.ShapeDty...]
where the time goes in v2:
time: 24 us; the launch traced here: 23.9 us
  Pallas kernels  22 us (92%)
  local copies, waits for them, and re-layouts  1.19 us (5%)
  between operations  0.64 us (3%)
    pallas_call x1, Pallas kernels, per_device(): pl.pallas_call(functools.partial(kernel, blocks), out_shape=(jax.ShapeDty...  22 us
    unnamed x2, local copies, waits for them, and re-layouts  1.19 us

profile of v2, /device:TPU:0, one launch (start us, length us, event | category | flops | bytes accessed | tf_op | source)
XLA Modules:
  0.0 23.9 jit_solution(15879979114859209561)
XLA Ops:
  0.6 22.0 %shard_map.104 = (f32[8,64]{1,0:T(8,128)S(1)}, f32[8,64]{1,0:T(8,128)S(1)}) custom-call(bf16[8,2,32,4096]{3,2,1,0:T(8,128)(2,1)} %x_hbm.1, bf16[8,2,32,4096]{3,2,1,0:T(8,128)(2,1)} %g_hbm.1, s32[8,32]{1,0:T(8,128)} %ids_hbm.1, s32[8,32]{1,0:T(8,128)} %codes_hbm.1, f32[16]{0:T(128)} %table_hbm.1, s32[4]{0:T(128)} %assign_hbm.1, bf16[4,64,4096]{2,1,0:T(8,128)(2,1)} %bin_hbm.1, ...), custom_call_target="tpu_custom_call" | custom-call | tf_op jit(solution)/shard_map/pallas_call | solution.py:309
  22.7 0.6 %copy.13 = f32[8,64]{1,0:T(8,128)} copy(f32[8,64]{1,0:T(8,128)S(1)} %get-tuple-element.4) | data formatting | bytes 4096
  23.3 0.6 %copy.14 = f32[8,64]{1,0:T(8,128)} copy(f32[8,64]{1,0:T(8,128)S(1)} %get-tuple-element.5) | data formatting | bytes 4096

commit v3 on v2

--- a/solution.py
+++ b/solution.py
@@ -22,10 +22,10 @@
 
 def kernel(
     blocks, x_hbm, g_hbm, ids_hbm, codes_hbm, table_hbm, assign_hbm, bin_hbm, bout_hbm, q_hbm,
-    scores_hbm, tangent_hbm,
+    terms,
     x_buf, g_buf, bin_buf, bout_buf, q_buf, in_own, kept_own, in_all, kept_all, kept_wide, grads, part, sums,
-    ids_ref, codes_ref, table_ref, assign_ref, result,
-    load_sem, basis_sem, q_send, q_recv, relay_send, in_send, kept_send, in_recv, kept_recv, sum_send, sum_recv, small_sem, result_sem,
+    ids_ref, codes_ref, table_ref, assign_ref,
+    load_sem, basis_sem, q_send, q_recv, relay_send, in_send, kept_send, in_recv, kept_recv, sum_send, sum_recv, small_sem,
 ):
     examples, slots, tokens, width = x_hbm.shape
     chips, rank = bin_hbm.shape[:2]
@@ -235,7 +235,7 @@
         q_buf[...].reshape(chips * q_buf.shape[1], features), grads[...], NT, preferred_element_type=jnp.float32
     )
     for place in range(chips * cores):
-        part[place] = scores[place * share : (place + 1) * share]
+        part[place, :, : count * kinds] = scores[place * share : (place + 1) * share]
 
     here = chip * cores + core
 
@@ -261,21 +261,19 @@
         for j in range(1, chips):
             total = total + sums[j * cores + c]
         by_core.append(total)
-    for kind in range(2):
-        result[kind] = jnp.concatenate(
-            [
-                total[:, at * kinds + kind * examples : at * kinds + (kind + 1) * examples]
-                for at in range(count)
-                for total in by_core
-            ],
-            axis=1,
-        )
-    results = [
-        pltpu.make_async_copy(result.at[kind], target, result_sem.at[kind])
-        for kind, target in enumerate((scores_hbm, tangent_hbm))
-    ]
-    for copy in results:
-        copy.start()
+    empty = jnp.zeros((share, examples), jnp.float32)
+    for c in range(cores):
+        for kind in range(2):
+            terms[c, kind] = jnp.concatenate(
+                [
+                    by_core[c][:, at * kinds + kind * examples : at * kinds + (kind + 1) * examples]
+                    if other == c
+                    else empty
+                    for at in range(count)
+                    for other in range(cores)
+                ],
+                axis=1,
+            )
 
     for k in range(slots):
 
@@ -289,8 +287,6 @@
         relay(h).wait_send()
     for other in range(1, chips * cores):
         sum_copy(other).wait_send()
-    for copy in results:
-        copy.wait()
 
 
 def per_device(blocks, x, g, ids, codes, table, assignment, basis_in, basis_out, query):
@@ -306,11 +302,12 @@
     hbm = pl.BlockSpec(memory_space=pltpu.HBM)
     bf16, f32 = jnp.bfloat16, jnp.float32
     dma = pltpu.SemaphoreType.DMA
-    return pl.pallas_call(
+    operands = (x, g, ids, codes, table, assignment, basis_in, basis_out, query)
+    terms = pl.pallas_call(
         functools.partial(kernel, blocks),
-        out_shape=(jax.ShapeDtypeStruct((share, count * cores * examples), f32),) * 2,
+        out_shape=jax.ShapeDtypeStruct((cores, 2, share, count * cores * examples), f32),
         in_specs=[hbm] * 9,
-        out_specs=(hbm, hbm),
+        out_specs=pl.BlockSpec(memory_space=pltpu.VMEM),
         scratch_shapes=[
             pltpu.VMEM((slots, examples, tokens, width), bf16),
             pltpu.VMEM((slots, examples, tokens, width), bf16),
@@ -323,13 +320,12 @@
             pltpu.VMEM((count, rank + 16, lanes), bf16),
             pltpu.VMEM((rank + 16, lanes), f32),
             pltpu.VMEM((count * kinds, features), bf16),
-            pltpu.VMEM((chips * cores, share, count * kinds), f32),
-            pltpu.VMEM((chips * cores, share, count * kinds), f32),
+            pltpu.VMEM((chips * cores, share, -(-count * kinds // 128) * 128), f32),
+            pltpu.VMEM((chips * cores, share, -(-count * kinds // 128) * 128), f32),
             pltpu.VMEM(ids.shape, jnp.int32),
             pltpu.VMEM(codes.shape, jnp.int32),
             pltpu.SMEM(table.shape, f32),
             pltpu.SMEM(assignment.shape, jnp.int32),
-            pltpu.VMEM((2, share, count * cores * examples), f32),
             dma((slots, 2)),
             dma((2,)),
             dma((slots,)),
@@ -342,12 +338,15 @@
             dma((chips * cores,)),
             dma((chips * cores,)),
             dma((4,)),
-            dma((2,)),
         ],
         compiler_params=pltpu.CompilerParams(
             collective_id=0, has_side_effects=True, vmem_limit_bytes=48 * 1024 * 1024
         ),
-    )(*[pltpu.with_memory_space_constraint(a, pltpu.HBM) for a in (x, g, ids, codes, table, assignment, basis_in, basis_out, query)])
+    )(*[pltpu.with_memory_space_constraint(operand, pltpu.HBM) for operand in operands])
+    both = terms[0]
+    for c in range(1, cores):
+        both = both + terms[c]
+    return both[0], both[1]
 
 
 def solution(mesh):

time: 24 us -> 23.4 us (0.975)
  local copies, waits for them, and re-layouts: 1.19 us -> 0.6 us
    unnamed x2 -> x0, local copies, waits for them, and re-layouts: 1.19 us -> none
    squeeze x0 -> x1, local copies, waits for them, and re-layouts: none -> 0.6 us  [per_device(): return (both[0], both[1])]
where the time goes in v3:
time: 23.4 us; the launch traced here: 23.2 us
  Pallas kernels  22 us (94%)
  between operations  0.65 us (3%)
  local copies, waits for them, and re-layouts  0.6 us (3%)
    pallas_call x1, Pallas kernels, per_device(): pl.pallas_call(functools.partial(kernel, blocks), out_shape=jax.ShapeDtyp...  22 us
    squeeze x1, local copies, waits for them, and re-layouts, per_device(): return (both[0], both[1])  0.6 us

profile of v3, /device:TPU:0, one launch (start us, length us, event | category | flops | bytes accessed | tf_op | source)
XLA Modules:
  0.0 23.2 jit_solution(2757325117176358043)
XLA Ops:
  0.6 22.0 %shard_map.104 = f32[2,2,8,64]{3,2,1,0:T(8,128)S(1)} custom-call(bf16[8,2,32,4096]{3,2,1,0:T(8,128)(2,1)} %x_hbm.1, bf16[8,2,32,4096]{3,2,1,0:T(8,128)(2,1)} %g_hbm.1, s32[8,32]{1,0:T(8,128)} %ids_hbm.1, s32[8,32]{1,0:T(8,128)} %codes_hbm.1, f32[16]{0:T(128)} %table_hbm.1, s32[4]{0:T(128)} %assign_hbm.1, bf16[4,64,4096]{2,1,0:T(8,128)(2,1)} %bin_hbm.1, ...), custom_call_target="tpu_custom_call" | custom-call | tf_op jit(solution)/shard_map/pallas_call | solution.py:306
  22.6 0.6 %slice_bitcast_fusion = (f32[8,64]{1,0:T(8,128)}, f32[8,64]{1,0:T(8,128)}) fusion(f32[1,2,8,64]{3,2,1,0:T(8,128)S(1)} %slice_add_fusion), kind=kLoop, calls=%fused_computation.1 | loop fusion | bytes 8192 | tf_op jit(solution)/shard_map/squeeze | solution.py:349
  (1 shorter events, 0.0 us)
